TPU v7x, 256 devices: a whole 4x4x8 slice. The times are simulated.
256 devices in a mesh: wide: 32 (over x, y, core), narrow: 8 (over z).
Axes of the slice: x: 4, y: 4, z: 8, core: 2. Of those that a mesh axis runs over, the one named last changes fastest.
Arguments:
- tokens: bfloat16 [16384, 4096], P('wide', 'narrow'), may hold values from -40 to 40
- norm_gain: float32 [4096], P('narrow'), may hold values from 0.5 to 5
- w_query: bfloat16 [4096, 4096], P(None, 'narrow'), may hold values from -0.09375 to 0.09375
- key_weight: bfloat16 [4096, 1024], P(None, 'narrow'), may hold values from -0.09375 to 0.09375
- value_weight: bfloat16 [4096, 1024], P(None, 'narrow'), may hold values from -0.09375 to 0.09375
- w_out: bfloat16 [4096, 4096], P('narrow'), may hold values from -0.09375 to 0.09375
- doc_lengths: int32 [64], replicated, may hold values from 1 to 8192, 16384 in all
Outputs:
- attended: bfloat16 [16384, 4096], P('wide', 'narrow')
Inputs may be any that keep to these rules, and one draw needn't show every extreme that they name: `doc_lengths`: the lengths sum to 16384; the longest is exactly 8192.
All inputs are finite; a program needn't handle non-finite values.
Results may differ from a plain program's by a relative error of at most 0.019.
The roundings to bfloat16 on the way count: a program that leaves them out, or rounds other values in their place, can miss the bound.
Values may be sent and summed in bfloat16 or wider, within the bound.
No kernel may reach another device: no remote copies, remote signals or barrier semaphores. Data moves between devices by JAX's collectives and lax.ppermute only.
A program may use at most 128 MiB of HBM per device.

v0:
```python
import math

import jax
import jax.numpy as jnp
from jax import lax
from jax.sharding import PartitionSpec as P

MODEL_WIDTH = 4096
HEAD_SIZE = 128


EPSILON = 1e-05
ROPE_BASE = 500000.0
NEGATIVE = -1e30


def doc_of(lengths, positions):
    starts = jnp.cumsum(lengths) - lengths
    return jnp.sum((starts[None, :] <= positions[:, None]).astype(jnp.int32), axis=1) - 1


def doc_info(lengths, positions):
    starts = jnp.cumsum(lengths) - lengths
    docs = doc_of(lengths, positions)
    onehot = docs[:, None] == jnp.arange(lengths.shape[0], dtype=jnp.int32)[None, :]
    first_tok = jnp.sum(jnp.where(onehot, starts[None, :], 0), axis=1)
    return (docs, positions - first_tok)


def apply_rotary(values, rotary_positions):
    half_width = values.shape[-1] // 2
    frequency = ROPE_BASE ** (-(jnp.arange(half_width, dtype=jnp.float32) * 2.0 / values.shape[-1]))
    angles = rotary_positions.astype(jnp.float32)[:, None] * frequency[None, :]
    cosine = jnp.cos(angles)[:, None, :]
    sine_part = jnp.sin(angles)[:, None, :]
    first_half = values[..., :half_width]
    second_half = values[..., half_width:]
    return jnp.concatenate(
        [
            first_half * cosine - second_half * sine_part,
            second_half * cosine + first_half * sine_part,
        ],
        axis=-1,
    )


def per_device(tokens, norm_gain, w_query, key_weight, value_weight, w_out, doc_lengths):
    tok_rows = tokens.shape[0]
    wide_index = lax.axis_index("wide")
    as_float = tokens.astype(jnp.float32)
    squares = lax.psum(jnp.sum(as_float * as_float, axis=1), "narrow")
    inverse = lax.rsqrt(squares / MODEL_WIDTH + EPSILON)
    normed = (as_float * inverse[:, None] * norm_gain[None, :]).astype(jnp.bfloat16)
    shard_piece = lax.all_gather(normed, "narrow", axis=1, tiled=True)
    query_raw, key_unrotated, value_projected = tuple(
        (
            jnp.dot(shard_piece, matrix, preferred_element_type=jnp.float32)
            for matrix in (w_query, key_weight, value_weight)
        )
    )
    positions = wide_index * tok_rows + jnp.arange(tok_rows, dtype=jnp.int32)
    own_doc, rotary_positions = doc_info(doc_lengths, positions)
    heads_local = w_query.shape[1] // HEAD_SIZE
    kv_local = key_weight.shape[1] // HEAD_SIZE
    heads_per_group = heads_local // kv_local
    queries_own = (
        apply_rotary(query_raw.reshape(tok_rows, heads_local, HEAD_SIZE), rotary_positions)
        .astype(jnp.bfloat16)
        .reshape(tok_rows, kv_local, heads_per_group, HEAD_SIZE)
    )
    rotated_keys = apply_rotary(
        key_unrotated.reshape(tok_rows, kv_local, HEAD_SIZE), rotary_positions
    ).astype(jnp.bfloat16)
    values_cast = value_projected.reshape(tok_rows, kv_local, HEAD_SIZE).astype(jnp.bfloat16)
    key_value = jnp.stack([rotated_keys, values_cast])
    score_scale = 1.0 / math.sqrt(HEAD_SIZE)
    last_pos = jnp.max(positions)
    first_doc = jnp.min(own_doc)

    def update(carried, key_tile, value_tile, key_pos, key_doc):
        run_max, run_sum, accum = carried
        scores = (
            jnp.einsum("rkgd,nkd->kgrn", queries_own, key_tile, preferred_element_type=jnp.float32)
            * score_scale
        )
        allowed = (key_doc[None, :] == own_doc[:, None]) & (key_pos[None, :] <= positions[:, None])
        masked = jnp.where(allowed, scores, NEGATIVE)
        new_max = jnp.maximum(run_max, jnp.max(masked, axis=-1))
        weights = jnp.where(allowed, jnp.exp(scores - new_max[..., None]), 0.0)
        factor = jnp.exp(run_max - new_max)
        run_sum = run_sum * factor + jnp.sum(weights, axis=-1)
        accum = accum * factor[..., None] + jnp.einsum(
            "kgrn,nkd->kgrd",
            weights.astype(jnp.bfloat16),
            value_tile,
            preferred_element_type=jnp.float32,
        )
        return (new_max, run_sum, accum)

    start_status = (
        jnp.full((kv_local, heads_per_group, tok_rows), NEGATIVE, jnp.float32),
        jnp.zeros((kv_local, heads_per_group, tok_rows), jnp.float32),
        jnp.zeros((kv_local, heads_per_group, tok_rows, HEAD_SIZE), jnp.float32),
    )
    pair = lax.all_gather(key_value, "wide", axis=1, tiled=True)
    count_keys = pair.shape[1]
    tile_width = math.gcd(count_keys, 512)
    tile_count = count_keys // tile_width

    def tile_step(tile_index, carried_in):
        offset = tile_index * tile_width
        key_tile = lax.dynamic_slice_in_dim(pair, offset, tile_width, 1)
        key_pos = offset + jnp.arange(tile_width, dtype=jnp.int32)
        key_doc = doc_of(doc_lengths, key_pos)
        needed = (key_pos[0] <= last_pos) & (key_doc[-1] >= first_doc)
        return lax.cond(
            needed,
            lambda status: update(status, key_tile[0], key_tile[1], key_pos, key_doc),
            lambda status: status,
            carried_in,
        )

    status_now = lax.fori_loop(0, tile_count, tile_step, start_status)
    run_max, run_sum, accum = status_now
    heads_out = (
        (accum / run_sum[..., None])
        .transpose(2, 0, 1, 3)
        .reshape(tok_rows, heads_local * HEAD_SIZE)
        .astype(jnp.bfloat16)
    )
    partial_out = jnp.dot(heads_out, w_out, preferred_element_type=jnp.float32)
    return lax.psum_scatter(
        partial_out.astype(jnp.bfloat16), "narrow", scatter_dimension=1, tiled=True
    )


def solution(mesh):
    in_specs = (
        P("wide", "narrow"),
        P("narrow"),
        P(None, "narrow"),
        P(None, "narrow"),
        P(None, "narrow"),
        P("narrow", None),
        P(),
    )
    out_specs = P("wide", "narrow")
    return jax.shard_map(
        per_device, mesh=mesh, in_specs=in_specs, out_specs=out_specs, check_vma=False
    )
```

profile of v0, /device:TPU:1, one launch (start us, length us, event | category | flops | bytes accessed | tf_op | source)
XLA Modules:
  0.0 502.1 jit_solution(14981264105822187456)
XLA Ops:
  6.5 1.3 fusion.25
  7.8 17.3 %psum.7 = f32[512]{0:T(512)S(1)} all-reduce(f32[512]{0:T(512)S(1)} %fusion.25), channel_id=1, replica_groups=mesh['wide'=32,'narrow'=8] {'narrow'}, use_global_device_ids=true, to_apply=%region_1.0 | all-reduce | flops 512 | bytes 4096 | tf_op jit(solution)/shard_map/psum | solution.py:51
  25.2 2.0 fusion.27
  27.3 0.8 copy.22
  28.3 0.7 sub.52
  29.1 0.7 broadcast_add_fusion.2
  29.9 54.0 %all-gather.3.cloned.1.call-done = bf16[512,4096]{1,0:T(8,128)(2,1)} async-done(((bf16[512,512]{1,0:T(8,128)(2,1)}), bf16[512,4096]{1,0:T(8,128)(2,1)}) %all-gather.3.cloned.1.call-update) | async-done | bytes 4194320 | tf_op jit(solution)/shard_map/all_gather | solution.py:54
  83.9 3.8 convolution_bitcast_fusion
  87.7 0.6 fusion.39
  88.3 1.5 fusion.24
  89.8 0.7 pad_maximum_fusion.1
  90.8 0.7 fusion.40
  91.5 1.7 multiply_cosine_fusion
  93.2 5.8 %fusion.43 = f32[512,512]{0,1:T(8,128)S(1)} fusion(bf16[512,4096]{1,0:T(8,128)(2,1)} %all-gather.3.cloned.1.call-done, bf16[4096,512]{1,0:T(8,128)(2,1)} %param.13), kind=kOutput, calls=%fused_computation.71 | convolution fusion | flops 2147483648 | bytes 9437184 | tf_op jit(solution)/shard_map/dot_general | solution.py:57
  99.1 0.9 fusion.42
  100.3 1.4 copy.31
  101.7 1.2 fusion.28
  103.2 51.1 %all-gather.5.cloned.1.call-done = bf16[2,16384,1,128]{1,3,2,0:T(8,128)(2,1)} async-done(((bf16[2,512,1,128]{1,3,2,0:T(8,128)(2,1)}), bf16[2,16384,1,128]{1,3,2,0:T(8,128)(2,1)}) %all-gather.5.cloned.1.call-update) | async-done | bytes 8388624 | tf_op jit(solution)/shard_map/all_gather | solution.py:105
  154.3 11.9 %copy.26 = bf16[2,16384,1,128]{3,1,2,0:T(8,128)(2,1)} copy(bf16[2,16384,1,128]{1,3,2,0:T(8,128)(2,1)} %all-gather.5.cloned.1.call-done) | data formatting | bytes 16777216
  166.3 134.6 %while.20 = (s32[]{:T(128)}, f32[1,4,512]{2,1,0:T(4,128)S(1)}, f32[1,4,512]{2,1,0:T(4,128)S(1)}, f32[1,4,512,128]{3,2,1,0:T(8,128)S(1)}, s32[]{:T(128)}, /*index...) while((s32[]{:T(128)}, f32[1,4,512]{2,1,0:T(4,128)S(1)}, ...), condition=%wide.region_13.14_spmd.clone, body=%wide.region_7.13_spmd.clone.sunk | while | flops 549821440 | bytes 33448608 | solution.py:123
  169.9 8.8 %conditional.3 = ((f32[1,4,512]{2,1,0:T(4,128)S(1)}, f32[1,4,512]{2,1,0:T(4,128)S(1)}, f32[1,4,512,128]{3,2,1,0:T(8,128)S(1)})) conditional(s32[]{:T(128)} %convert_element_type.114, (f32[1,4,512]{2,1,0:T(4,128)S(1)}, f32[1,4,512]{2,1,0:T(4,128)S(1)}, f32[1,4,512,128]{3,2,1,0:T(8,128)S(1)}) %tuple.65, (s32[512]{0:T(512)S(1)}, s32[512]{0:T(512)S(1)}, ...), branch_computations={%region_9.9_spmd, %region_10.12_spmd} | conditional | flops 549722624 | bytes 33435770 | solution.py:116
  170.2 3.7 fusion.2
  174.0 3.8 fusion.14
  177.8 0.9 fusion.6
  182.4 8.8 %conditional.3 = ((f32[1,4,512]{2,1,0:T(4,128)S(1)}, f32[1,4,512]{2,1,0:T(4,128)S(1)}, f32[1,4,512,128]{3,2,1,0:T(8,128)S(1)})) conditional(s32[]{:T(128)} %convert_element_type.114, (f32[1,4,512]{2,1,0:T(4,128)S(1)}, f32[1,4,512]{2,1,0:T(4,128)S(1)}, f32[1,4,512,128]{3,2,1,0:T(8,128)S(1)}) %tuple.65, (s32[512]{0:T(512)S(1)}, s32[512]{0:T(512)S(1)}, ...), branch_computations={%region_9.9_spmd, %region_10.12_spmd} | conditional | flops 549722624 | bytes 33435770 | solution.py:116
  182.7 3.7 fusion.2
  186.5 3.8 fusion.14
  190.3 0.9 fusion.6
  300.9 1.3 copy.27
  302.2 1.4 divide_convert_fusion
  303.6 6.5 %convolution_convert_fusion = bf16[512,4096]{1,0:T(8,128)(2,1)} fusion(bf16[512,512]{0,1:T(8,128)(2,1)S(1)} %bitcast.96, bf16[512,4096]{1,0:T(8,128)(2,1)} %param.16), kind=kOutput, calls=%fused_computation.30 | convolution fusion | flops 2149580800 | bytes 8912896 | tf_op jit(solution)/shard_map/dot_general | solution.py:131
  310.1 185.5 %reduce-scatter.2.cloned.1.call-done = bf16[512,512]{1,0:T(8,128)(2,1)} async-done(((bf16[512,4096]{1,0:T(8,128)(2,1)}), bf16[512,512]{1,0:T(8,128)(2,1)}) %reduce-scatter.2.cloned.1.call-update) | async-done | bytes 524304 | tf_op jit(solution)/shard_map/reduce_scatter | solution.py:132
  (261 shorter events, 39.1 us)
Async XLA Ops:
  6.5 77.4 %copy-start = (bf16[4096,128]{1,0:T(8,128)(2,1)S(1)}, bf16[4096,128]{1,0:T(8,128)(2,1)}, u32[]{:S(2)}) copy-start(bf16[4096,128]{1,0:T(8,128)(2,1)} %param.14) | copy-start | bytes 3145732
  6.5 77.4 %all-gather.3.cloned.1.call-start = ((), (), s32[]{:S(2)}) async-start(), calls=%async_computation.1 | async-start | bytes 4718592 | tf_op jit(solution)/shard_map/all_gather | solution.py:54
  27.2 61.1 %copy-start.3 = (bf16[4096,128]{1,0:T(8,128)(2,1)S(1)}, bf16[4096,128]{1,0:T(8,128)(2,1)}, u32[]{:S(2)}) copy-start(bf16[4096,128]{1,0:T(8,128)(2,1)} %param.15) | copy-start | bytes 3145732
  27.2 127.1 %all-gather.5.cloned.1.call-start = ((), (), s32[]{:S(2)}) async-start(), calls=%async_computation.2 | async-start | bytes 8650752 | tf_op jit(solution)/shard_map/all_gather | solution.py:105
  83.9 4.4 copy-start.2
  90.6 405.0 %reduce-scatter.2.cloned.1.call-start = ((), (), s32[]{:S(2)}) async-start(), calls=%async_computation.3 | async-start | bytes 4718592 | tf_op jit(solution)/shard_map/reduce_scatter | solution.py:132
  174.0 3.8 copy-start.1
  186.5 3.8 copy-start.1
Sparse Core Ops, SparseCore 0:
  27.3 56.5 all-gather.2
  90.7 63.5 all-gather.4
  310.2 185.3 reduce-scatter.1
where the time goes:
time: 505 us; the launch traced here: 502 us
  waiting for transfers between devices  291 us (58%)
  loops' own time  80.4 us (16%)
  local copies, waits for them, and re-layouts  50.1 us (10%)
  matrix products  32.8 us (6%)
  other arithmetic  17.4 us (3%)
  blocking collectives  17.3 us (3%)
  between operations  13.2 us (3%)
    reduce_scatter x1, waiting for transfers between devices, per_device(): lax.psum_scatter(partial_out.astype(jnp.bfloat16), 'narrow', scatter_dime...  185 us
    another operation x1, loops' own time, per_device(): status_now = lax.fori_loop(0, tile_count, tile_step, start_status)  79.9 us
    all_gather x1, waiting for transfers between devices, per_device(): shard_piece = lax.all_gather(normed, 'narrow', axis=1, tiled=True)  54 us
    all_gather x1, waiting for transfers between devices, per_device(): pair = lax.all_gather(key_value, 'wide', axis=1, tiled=True)  51.1 us
    slice x64, local copies, waits for them, and re-layouts, tile_step(): needed = (key_pos[0] <= last_pos) & (key_doc[-1] >= first_doc)  33.3 us
    psum x1, blocking collectives, per_device(): squares = lax.psum(jnp.sum(as_float * as_float, axis=1), 'narrow')  17.3 us
    unnamed x9, local copies, waits for them, and re-layouts  13.6 us
    dot_general x3, matrix products, per_device(): jnp.dot(shard_piece, matrix, preferred_element_type=jnp.float32)  11.2 us
  transfers between devices with their start and end apart: 3, of which 3 were waited for; matrix products, arithmetic and copies ran while one was open for 3% of the time, Pallas kernels for 0%

commit v1 on v0

v1 whole, which is shorter than its diff:
```python
import functools
import math

import jax
import jax.numpy as jnp
from jax import lax
from jax.experimental import pallas as pl
from jax.experimental.pallas import tpu as pltpu
from jax.sharding import PartitionSpec as P

MODEL_WIDTH = 4096
HEAD_SIZE = 128
EPSILON = 1e-05
ROPE_BASE = 500000.0
NEGATIVE = -1e30
VMEM_LIMIT = 56 * 1024 * 1024

_NT = (((1,), (1,)), ((), ()))


def project_kernel(x_ref, gain_ref, w_ref, cos_ref, sin_ref, q_ref, k_ref, vt_ref):
    x = x_ref[...].astype(jnp.float32)
    squares = jnp.sum(x * x, axis=1, keepdims=True)
    inverse = lax.rsqrt(squares / MODEL_WIDTH + EPSILON)
    normed = (x * inverse * gain_ref[...]).astype(jnp.bfloat16)
    raw = jnp.dot(normed, w_ref[...], preferred_element_type=jnp.float32)
    cos, sin = cos_ref[...], sin_ref[...]
    heads = q_ref.shape[0]
    for h in range(heads + 1):
        part = raw[:, h * HEAD_SIZE : (h + 1) * HEAD_SIZE]
        turned = (part * cos + pltpu.roll(part, HEAD_SIZE // 2, 1) * sin).astype(jnp.bfloat16)
        if h < heads:
            q_ref[h] = turned
        else:
            k_ref[...] = turned
    vt_ref[...] = raw[:, (heads + 1) * HEAD_SIZE :].T.astype(jnp.bfloat16)


def project(x, gain, weights, cos, sin, heads):
    rows = x.shape[0]
    block = math.gcd(rows, 128)
    width = weights.shape[1]
    return pl.pallas_call(
        project_kernel,
        grid=(rows // block,),
        in_specs=[
            pl.BlockSpec((block, MODEL_WIDTH), lambda i: (i, 0)),
            pl.BlockSpec((1, MODEL_WIDTH), lambda i: (0, 0)),
            pl.BlockSpec((MODEL_WIDTH, width), lambda i: (0, 0)),
            pl.BlockSpec((block, HEAD_SIZE), lambda i: (i, 0)),
            pl.BlockSpec((block, HEAD_SIZE), lambda i: (i, 0)),
        ],
        out_specs=[
            pl.BlockSpec((heads, block, HEAD_SIZE), lambda i: (0, i, 0)),
            pl.BlockSpec((block, HEAD_SIZE), lambda i: (i, 0)),
            pl.BlockSpec((HEAD_SIZE, block), lambda i: (0, i)),
        ],
        out_shape=[
            jax.ShapeDtypeStruct((heads, rows, HEAD_SIZE), jnp.bfloat16),
            jax.ShapeDtypeStruct((rows, HEAD_SIZE), jnp.bfloat16),
            jax.ShapeDtypeStruct((HEAD_SIZE, rows), jnp.bfloat16),
        ],
        compiler_params=pltpu.CompilerParams(vmem_limit_bytes=VMEM_LIMIT),
        cost_estimate=pl.CostEstimate(
            flops=2 * rows * MODEL_WIDTH * width,
            bytes_accessed=2 * (rows * MODEL_WIDTH + MODEL_WIDTH * width),
            transcendentals=0,
        ),
        name="norm_project",
    )(x, gain, weights, cos, sin)


def attend_kernel(
    tile, info_ref, first_ref, q_ref, k_hbm, vt_hbm, w_hbm, out_hbm,
    k_buf, v_buf, w_buf, out_buf, top_ref, total_ref, mix_ref, k_sem, v_sem, w_sem, out_sem,
):
    low, own, base, late = info_ref[0], info_ref[1], info_ref[2], info_ref[3]
    heads, rows = q_ref.shape[0], q_ref.shape[1]
    factor = math.log2(math.e) / math.sqrt(HEAD_SIZE)

    def key_copy(j):
        return pltpu.make_async_copy(k_hbm.at[j], k_buf.at[j], k_sem.at[j])

    def value_copy(j):
        return pltpu.make_async_copy(vt_hbm.at[j], v_buf.at[j], v_sem.at[j])

    def start(j):
        key_copy(j).start()
        value_copy(j).start()

    start(own)
    lax.fori_loop(low, own, lambda j, _: (start(j), 0)[1], 0)
    w_copy = pltpu.make_async_copy(w_hbm, w_buf, w_sem)
    w_copy.start()

    top_ref[...] = jnp.full(top_ref.shape, NEGATIVE, jnp.float32)
    total_ref[...] = jnp.zeros(total_ref.shape, jnp.float32)
    mix_ref[...] = jnp.zeros(mix_ref.shape, jnp.float32)

    def step(j, masked):
        keys, values = k_buf[j], v_buf[j]
        if masked:
            key_pos = j * tile + lax.broadcasted_iota(jnp.int32, (tile, rows), 0)
            query_pos = base + lax.broadcasted_iota(jnp.int32, (tile, rows), 1)
            allowed = (key_pos >= first_ref[...]) & (key_pos <= query_pos)
        for h in range(heads):
            scores = lax.dot_general(keys, q_ref[h], _NT, preferred_element_type=jnp.float32)
            if masked:
                scores = jnp.where(allowed, scores, NEGATIVE)
            old = top_ref[h]
            new = jnp.maximum(old, jnp.max(scores, axis=0, keepdims=True))
            weights = jnp.exp2(scores * factor - new * factor)
            shrink = jnp.exp2((old - new) * factor)
            top_ref[h] = new
            total_ref[h] = total_ref[h] * shrink + jnp.sum(weights, axis=0, keepdims=True)
            mix_ref[h] = mix_ref[h] * shrink + jnp.dot(
                values, weights.astype(jnp.bfloat16), preferred_element_type=jnp.float32
            )

    def visit(j):
        key_copy(j).wait()
        value_copy(j).wait()
        clear = (j * tile >= late) & (j * tile + tile - 1 <= base)

        @pl.when(clear)
        def _():
            step(j, False)

        @pl.when(jnp.logical_not(clear))
        def _():
            step(j, True)

    visit(own)
    lax.fori_loop(low, own, lambda j, _: (visit(j), 0)[1], 0)

    mixed = jnp.concatenate(
        [(mix_ref[h] / total_ref[h]).T.astype(jnp.bfloat16) for h in range(heads)], axis=1
    )
    w_copy.wait()
    count = out_sem.shape[0]
    width = out_buf.shape[1] // count
    copies = []
    for n in range(count):
        columns = pl.ds(n * width, width)
        out_buf[:, columns] = jnp.dot(
            mixed, w_buf[:, columns], preferred_element_type=jnp.float32
        ).astype(jnp.bfloat16)
        copy = pltpu.make_async_copy(out_buf.at[:, columns], out_hbm.at[:, columns], out_sem.at[n])
        copy.start()
        copies.append(copy)
    for copy in copies:
        copy.wait()


def attend(info, first, q, keys, values, w_out):
    heads, rows, _ = q.shape
    tiles, tile, _ = keys.shape
    width = w_out.shape[1]
    anywhere = pl.BlockSpec(memory_space=pl.ANY)
    vmem = pl.BlockSpec(memory_space=pltpu.VMEM)
    return pl.pallas_call(
        functools.partial(attend_kernel, tile),
        in_specs=[pl.BlockSpec(memory_space=pltpu.SMEM), vmem, vmem, anywhere, anywhere, anywhere],
        out_specs=anywhere,
        out_shape=jax.ShapeDtypeStruct((rows, width), jnp.bfloat16),
        scratch_shapes=[
            pltpu.VMEM(keys.shape, jnp.bfloat16),
            pltpu.VMEM(values.shape, jnp.bfloat16),
            pltpu.VMEM(w_out.shape, jnp.bfloat16),
            pltpu.VMEM((rows, width), jnp.bfloat16),
            pltpu.VMEM((heads, 1, rows), jnp.float32),
            pltpu.VMEM((heads, 1, rows), jnp.float32),
            pltpu.VMEM((heads, HEAD_SIZE, rows), jnp.float32),
            pltpu.SemaphoreType.DMA((tiles,)),
            pltpu.SemaphoreType.DMA((tiles,)),
            pltpu.SemaphoreType.DMA,
            pltpu.SemaphoreType.DMA((4,)),
        ],
        compiler_params=pltpu.CompilerParams(vmem_limit_bytes=VMEM_LIMIT),
        cost_estimate=pl.CostEstimate(
            flops=4 * heads * rows * HEAD_SIZE * tiles * tile // 2,
            bytes_accessed=2 * (keys.size + values.size + w_out.size),
            transcendentals=heads * rows * tiles * tile // 2,
        ),
        name="attend",
    )(info, first, q, keys, values, w_out)


def per_device(tokens, norm_gain, w_query, key_weight, value_weight, w_out, doc_lengths):
    rows = tokens.shape[0]
    wide_index = lax.axis_index("wide")
    heads = w_query.shape[1] // HEAD_SIZE

    full = lax.all_gather(tokens, "narrow", axis=1, tiled=True)
    gain = lax.all_gather(norm_gain, "narrow", axis=0, tiled=True)
    weights = jnp.concatenate([w_query, key_weight, value_weight], axis=1)

    with jax.named_scope("positions"):
        docs = doc_lengths.shape[0]
        earlier = jnp.arange(docs)[None, :] < jnp.arange(docs)[:, None]
        starts = jnp.sum(jnp.where(earlier, doc_lengths[None, :], 0), axis=1)
        base = wide_index * rows
        positions = base + jnp.arange(rows, dtype=jnp.int32)
        first = jnp.max(
            jnp.where(starts[None, :] <= positions[:, None], starts[None, :], 0), axis=1
        ).astype(jnp.int32)
        half = HEAD_SIZE // 2
        frequency = ROPE_BASE ** (-(jnp.arange(half, dtype=jnp.float32) * 2.0 / HEAD_SIZE))
        angles = (positions - first).astype(jnp.float32)[:, None] * frequency[None, :]
        cosine, sine = jnp.cos(angles), jnp.sin(angles)
        cos = jnp.concatenate([cosine, cosine], axis=1)
        sin = jnp.concatenate([-sine, sine], axis=1)
        info = jnp.stack([first[0] // rows, wide_index, base, first[-1]]).astype(jnp.int32)

    q, k, vt = project(full, gain.reshape(1, -1), weights, cos, sin, heads)
    keys = lax.all_gather(k, "wide", axis=0)
    values = lax.all_gather(vt, "wide", axis=0)
    partial_out = attend(info, first.reshape(1, -1), q, keys, values, w_out)
    return lax.psum_scatter(partial_out, "narrow", scatter_dimension=1, tiled=True)


def solution(mesh):
    in_specs = (
        P("wide", "narrow"),
        P("narrow"),
        P(None, "narrow"),
        P(None, "narrow"),
        P(None, "narrow"),
        P("narrow", None),
        P(),
    )
    return jax.shard_map(
        per_device, mesh=mesh, in_specs=in_specs, out_specs=P("wide", "narrow"), check_vma=False
    )
```

time: 505 us -> 288 us (0.57)
  loops' own time: 80.4 us -> 0 us
  waiting for transfers between devices: 291 us -> 220 us
  local copies, waits for them, and re-layouts: 50.1 us -> 0.62 us
  matrix products: 32.8 us -> 0 us
  Pallas kernels: 0 us -> 20.5 us
  other arithmetic: 17.4 us -> 10.6 us
    reduce_scatter x1, waiting for transfers between devices: 185 us -> 89.8 us  [per_device(): lax.psum_scatter(partial_out, 'narrow', scatter_dimension=1, tiled=True)]
    another operation x33 -> x0, loops' own time: 80.4 us -> none  [the longest x1 79.9 us: per_device(): status_now = lax.fori_loop(0, tile_count, tile_step, start_status)]
    slice x65 -> x1, local copies, waits for them, and re-layouts: 34.2 us -> 0.61 us  [per_device(): first[0] // rows]
    dot_general x8 -> x0, matrix products: 32.8 us -> none  [the longest x3 11.2 us: per_device(): jnp.dot(shard_piece, matrix, preferred_element_type=jnp.float32)]
    all_gather x2 -> x3, waiting for transfers between devices: 105 us -> 129 us  [the longest x1 53.1 us: per_device(): values = lax.all_gather(vt, 'wide', axis=0)]
    all_gather x0 -> x1, blocking collectives: none -> 20.6 us  [per_device(): gain = lax.all_gather(norm_gain, 'narrow', axis=0, tiled=True)]
    pallas_call x0 -> x2, Pallas kernels: none -> 20.5 us  [the longest x1 11 us: attend(): pl.pallas_call(functools.partial(attend_kernel, tile), in_specs=[pl.Block...]
    psum x1 -> x0, blocking collectives: 17.3 us -> none  [per_device(): squares = lax.psum(jnp.sum(as_float * as_float, axis=1), 'narrow')]
  transfers between devices with their start and end apart: 3 -> 4, of which waited for: 3 -> 4; matrix products, arithmetic and copies ran while one was open for 3% -> 4% of each run, Pallas kernels for 0% -> 0%
where the time goes in v1:
time: 288 us
  waiting for transfers between devices  220 us (76%)
  blocking collectives  20.6 us (7%)
  Pallas kernels  20.5 us (7%)
  between operations  15.7 us (5%)
  other arithmetic  10.6 us (4%)
    reduce_scatter x1, waiting for transfers between devices, per_device(): lax.psum_scatter(partial_out, 'narrow', scatter_dimension=1, tiled=True)  89.8 us
    all_gather x1, waiting for transfers between devices, per_device(): values = lax.all_gather(vt, 'wide', axis=0)  53.1 us
    all_gather x1, waiting for transfers between devices, per_device(): keys = lax.all_gather(k, 'wide', axis=0)  45 us
    all_gather x1, waiting for transfers between devices, per_device(): full = lax.all_gather(tokens, 'narrow', axis=1, tiled=True)  30.6 us
    all_gather x1, blocking collectives, per_device(): gain = lax.all_gather(norm_gain, 'narrow', axis=0, tiled=True)  20.6 us
    pallas_call x1, Pallas kernels, attend(): pl.pallas_call(functools.partial(attend_kernel, tile), in_specs=[pl.Block...  11 us
    pallas_call x1, Pallas kernels, project(): pl.pallas_call(project_kernel, grid=(rows // block,), in_specs=[pl.BlockS...  9.54 us
    concatenate x1, other arithmetic, per_device(): weights = jnp.concatenate([w_query, key_weight, value_weight], axis=1)  6.46 us
  transfers between devices with their start and end apart: 4, of which 4 were waited for; matrix products, arithmetic and copies ran while one was open for 4% of the time, Pallas kernels for 0%

profile of v1, /device:TPU:1, one launch (start us, length us, event | category | flops | bytes accessed | tf_op | source)
XLA Modules:
  0.0 288.1 jit_solution(9651233907600724789)
XLA Ops:
  6.5 0.0 all-gather.7.cloned.1.call-start
  6.5 0.7 all-gather.7.cloned.1.call-update
  7.3 0.0 all-gather.9.cloned.1.call-start
  7.3 20.6 %all-gather.2 = f32[8,1,512]{2,1,0:T(1,128)} all-gather(f32[1,1,512]{2,1,0:T(1,128)} %bitcast.11), channel_id=1, replica_groups=mesh['wide'=32,'narrow'=8] {'narrow'}, dimensions={0}, use_global_device_ids=true | all-gather | bytes 18432 | tf_op jit(solution)/shard_map/all_gather | solution.py:195
  27.9 0.8 select_reduce_fusion.1
  28.7 0.1 select_reduce_fusion
  28.8 0.0 copy-start
  28.8 1.0 fusion
  29.8 1.0 pad_maximum_fusion.1
  30.9 6.5 %pad_maximum_fusion.w_ref = bf16[4096,768]{1,0:T(8,128)(2,1)} fusion(bf16[4096,128]{1,0:T(8,128)(2,1)} %param.11, bf16[4096,128]{1,0:T(8,128)(2,1)} %param.10, bf16[4096,512]{1,0:T(8,128)(2,1)} %param.9), kind=kLoop, calls=%fused_computation | loop fusion | flops 18874368 | bytes 12582912 | tf_op jit(solution)/shard_map/concatenate | solution.py:196
  37.3 30.6 %all-gather.7.cloned.1.call-done.x_ref = bf16[512,4096]{1,0:T(8,128)(2,1)} async-done(((bf16[512,512]{1,0:T(8,128)(2,1)}), bf16[512,4096]{1,0:T(8,128)(2,1)}) %all-gather.7.cloned.1.call-update) | async-done | bytes 4194320 | tf_op jit(solution)/shard_map/all_gather | solution.py:194
  67.9 9.5 %norm_project.1 = (bf16[4,512,128]{2,1,0:T(8,128)(2,1)}, bf16[512,128]{1,0:T(8,128)(2,1)}, bf16[128,512]{1,0:T(8,128)(2,1)}) custom-call(bf16[512,4096]{1,0:T(8,128)(2,1)} %all-gather.7.cloned.1.call-done.x_ref, f32[1,4096]{1,0:T(1,128)} %bitcast.9, bf16[4096,768]{1,0:T(8,128)(2,1)} %pad_maximum_fusion.w_ref, f32[512,128]{1,0:T(8,128)} %get-tuple-element.16.cos_ref, ...), custom_call_target="tpu_custom_call" | custom-call | flops 3221225472 | bytes 10485760 | tf_op jit(solution)/shard_map/norm_project/pallas_call | solution.py:43
  77.4 0.0 all-gather.9.cloned.1.call-update
  77.5 0.0 all-gather.11.cloned.1.call-start
  77.5 0.7 all-gather.11.cloned.1.call-update
  78.2 0.0 reduce-scatter.2.cloned.1.call-start
  78.2 0.0 copy-done
  78.3 0.6 fusion.1
  81.4 1.2 pad_add_fusion.info_ref
  82.6 45.0 %all-gather.9.cloned.1.call-done = bf16[16384,128]{1,0:T(8,128)(2,1)} async-done(((bf16[512,128]{1,0:T(8,128)(2,1)}), bf16[16384,128]{1,0:T(8,128)(2,1)}) %all-gather.9.cloned.1.call-update) | async-done | bytes 4194320 | tf_op jit(solution)/shard_map/all_gather | solution.py:216
  127.7 53.1 %all-gather.11.cloned.1.call-done = bf16[4096,512]{1,0:T(8,128)(2,1)} async-done(((bf16[128,512]{1,0:T(8,128)(2,1)}), bf16[4096,512]{1,0:T(8,128)(2,1)}) %all-gather.11.cloned.1.call-update) | async-done | bytes 4194320 | tf_op jit(solution)/shard_map/all_gather | solution.py:217
  180.8 11.0 %attend.1 = bf16[512,4096]{1,0:T(8,128)(2,1)} custom-call(s32[4]{0:T(128)} %pad_add_fusion.info_ref, s32[1,512]{1,0:T(1,128)} %bitcast.10, bf16[4,512,128]{2,1,0:T(8,128)(2,1)} %get-tuple-element.8.q_ref, bf16[32,512,128]{2,1,0:T(8,128)(2,1)} %bitcast.12, bf16[32,128,512]{2,1,0:T(8,128)(2,1)} %bitcast.13, bf16[512,4096]{1,0:T(8,128)(2,1)} %w_hbm.1), custom_call_target="tpu_custom_call" | custom-call | flops 8589934592 | bytes 12582912 | tf_op jit(solution)/shard_map/attend/pallas_call | solution.py:161
  191.7 0.0 reduce-scatter.2.cloned.1.call-update
  191.8 89.8 %reduce-scatter.2.cloned.1.call-done = bf16[512,512]{1,0:T(8,128)(2,1)} async-done(((bf16[512,4096]{1,0:T(8,128)(2,1)}), bf16[512,512]{1,0:T(8,128)(2,1)}) %reduce-scatter.2.cloned.1.call-update) | async-done | bytes 524304 | tf_op jit(solution)/shard_map/reduce_scatter | solution.py:219
  (3 shorter events, 0.0 us)
Async XLA Ops:
  6.5 61.4 %all-gather.7.cloned.1.call-start = ((), (), s32[]{:S(2)}) async-start(), calls=%async_computation.1 | async-start | bytes 4718592 | tf_op jit(solution)/shard_map/all_gather | solution.py:194
  7.3 120.4 %all-gather.9.cloned.1.call-start = ((), (), s32[]{:S(2)}) async-start(), calls=%async_computation.3 | async-start | bytes 4325376 | tf_op jit(solution)/shard_map/all_gather | solution.py:216
  28.8 49.4 %copy-start = (s32[512]{0:T(512)}, s32[512]{0:T(512)S(1)}, u32[]{:S(2)}) copy-start(s32[512]{0:T(512)S(1)} %select_reduce_fusion) | copy-start | bytes 6148
  77.5 103.3 %all-gather.11.cloned.1.call-start = ((), (), s32[]{:S(2)}) async-start(), calls=%async_computation.4 | async-start | bytes 4325376 | tf_op jit(solution)/shard_map/all_gather | solution.py:217
  78.2 203.3 %reduce-scatter.2.cloned.1.call-start = ((), (), s32[]{:S(2)}) async-start(), calls=%async_computation.2 | async-start | bytes 4718592 | tf_op jit(solution)/shard_map/reduce_scatter | solution.py:219
Sparse Core Ops, SparseCore 0:
  9.1 58.6 all-gather.6
  77.6 50.0 all-gather.8
  130.2 50.5 all-gather.10
  191.9 89.5 reduce-scatter.1
